TPU v7x, 32 devices: a whole 2x2x4 slice. The times are simulated.
32 devices in a mesh: clips: 2 (over y), rows: 8 (over z, x), kern: 2 (over core).
Axes of the slice: x: 2, y: 2, z: 4, core: 2. Of those that a mesh axis runs over, the one named last changes fastest.
Arguments:
- features: bfloat16 [16, 512, 256], P('kern', ('clips', 'rows')), parts along dimension 1, may hold values from -6 to 6
- head_weight: float32 [16], P('kern'), may hold values from -1.5 to 1.5
- kernels: float32 [8, 2, 128, 128], P('kern')
- kernel_weights: float32 [8], P('kern'), may hold values from 0.25 to 2
- target: bfloat16 [512, 256], P(('clips', 'rows')), parts along dimension 0, may hold values from 0 to 1
Outputs:
- grad_features: bfloat16 [16, 512, 256], P('kern', ('clips', 'rows')), parts along dimension 1
There are 2 independent parts, one for each index of `clips`. A program takes and returns all parts, laid end to end along the dimension named above; an argument that names none is the same for every part. Nothing has to cross between parts.
All inputs are finite; a program needn't handle non-finite values.
Results may differ from a plain program's by a relative error of at most 0.001.
Values sent between devices are 32-bit elements; how exact they have to be, the bound alone decides.
A program may use at most 64 MiB of HBM per device.

v0:
```python
import math

import jax
import jax.numpy as jnp
from jax import lax
from jax.sharding import PartitionSpec as P

precise = lax.Precision.HIGHEST
steepness = 2.0
threshold = 2.0


def band_tables(row_ids, band_len, full_len):
    frequency = jnp.arange(band_len, dtype=jnp.int32) - band_len // 2
    phases = jnp.mod(row_ids[:, None] * frequency[None, :], full_len)
    angles = phases.astype(jnp.float32) * (2.0 * math.pi / full_len)
    return (jnp.cos(angles), jnp.sin(angles))


def right_prod(lhs_part, lookup):
    return jnp.dot(lhs_part, lookup, precision=precise, preferred_element_type=jnp.float32)


def right_trans(lhs_part, lookup):
    return lax.dot_general(
        lhs_part,
        lookup,
        (((1,), (1,)), ((), ())),
        precision=precise,
        preferred_element_type=jnp.float32,
    )


def batch_left(lookup, blocks):
    return jnp.einsum(
        "rs,krt->kst", lookup, blocks, precision=precise, preferred_element_type=jnp.float32
    )


def batch_apply(lookup, blocks):
    return jnp.einsum(
        "rs,kst->krt", lookup, blocks, precision=precise, preferred_element_type=jnp.float32
    )


def synthesize(filt_real, filt_imag, cos_rows, sin_rows, cos_full, sin_full):
    kern_count = filt_real.shape[0]
    band_len = filt_real.shape[-1]
    row_count = cos_rows.shape[0]
    q_real = (batch_apply(cos_rows, filt_real) - batch_apply(sin_rows, filt_imag)).reshape(
        kern_count * row_count, band_len
    )
    q_imag = (batch_apply(cos_rows, filt_imag) + batch_apply(sin_rows, filt_real)).reshape(
        kern_count * row_count, band_len
    )
    out_real = (right_trans(q_real, cos_full) - right_trans(q_imag, sin_full)) / band_len
    out_imag = (right_trans(q_real, sin_full) + right_trans(q_imag, cos_full)) / band_len
    return (
        out_real.reshape(kern_count, row_count, -1),
        out_imag.reshape(kern_count, row_count, -1),
    )


def analyze(grad_real, grad_imag, cos_rows, sin_rows, cos_full, sin_full):
    kern_count, row_count, full_len = grad_real.shape
    band_len = cos_full.shape[1]
    flat_real = grad_real.reshape(kern_count * row_count, full_len)
    flat_imag = grad_imag.reshape(kern_count * row_count, full_len)
    b_real = (right_prod(flat_real, cos_full) + right_prod(flat_imag, sin_full)).reshape(
        kern_count, row_count, band_len
    )
    b_imag = (right_prod(flat_imag, cos_full) - right_prod(flat_real, sin_full)).reshape(
        kern_count, row_count, band_len
    )
    dy_real = (batch_left(cos_rows, b_real) + batch_left(sin_rows, b_imag)) / band_len
    dy_imag = (batch_left(cos_rows, b_imag) - batch_left(sin_rows, b_real)) / band_len
    return (dy_real, dy_imag)


def conj_combine(kernels, dy_real, dy_imag):
    gain_real = kernels[:, 0]
    gain_imag = kernels[:, 1]
    dx_real = jnp.sum(gain_real * dy_real + gain_imag * dy_imag, axis=0)
    dx_imag = jnp.sum(gain_real * dy_imag - gain_imag * dy_real, axis=0)
    return (dx_real, dx_imag)


def band_part(mask_map, cos_rows, sin_rows, cos_full, sin_full):
    half_real = right_prod(mask_map, cos_full)
    half_imag = -right_prod(mask_map, sin_full)
    part_real = (batch_left(cos_rows, half_real[None]) + batch_left(sin_rows, half_imag[None]))[0]
    part_imag = (batch_left(cos_rows, half_imag[None]) - batch_left(sin_rows, half_real[None]))[0]
    return (part_real, part_imag)


def filter_all(kernels, spec_real, spec_imag):
    gain_real = kernels[:, 0]
    gain_imag = kernels[:, 1]
    filt_real = gain_real * spec_real[None] - gain_imag * spec_imag[None]
    filt_imag = gain_real * spec_imag[None] + gain_imag * spec_real[None]
    return (filt_real, filt_imag)


def resist_grad(intensity, target_rows):
    resist = jax.nn.sigmoid(steepness * (intensity - threshold))
    return 2.0 * (resist - target_rows.astype(jnp.float32)) * steepness * resist * (1.0 - resist)


def back_rows(grad_real, grad_imag, cos_rows, sin_rows, cos_full, sin_full, mask_map):
    full_len = cos_full.shape[0]
    q_real = right_prod(cos_rows, grad_real) - right_prod(sin_rows, grad_imag)
    q_imag = right_prod(cos_rows, grad_imag) + right_prod(sin_rows, grad_real)
    grad_mask = (right_trans(q_real, cos_full) - right_trans(q_imag, sin_full)) / full_len
    return grad_mask * mask_map * (1.0 - mask_map)


def on_device(features, head_weight, kernels, kernel_weights, target):
    row_count = target.shape[0]
    full_len = target.shape[1]
    band_len = kernels.shape[-1]
    cos_full, sin_full = band_tables(jnp.arange(full_len, dtype=jnp.int32), band_len, full_len)
    local_logits = jnp.sum(head_weight[:, None, None] * features.astype(jnp.float32), axis=0)
    row_ids = lax.axis_index("rows") * row_count + jnp.arange(row_count, dtype=jnp.int32)
    cos_rows, sin_rows = band_tables(row_ids, band_len, full_len)
    logits = lax.psum(local_logits, "kern")
    mask_map = jax.nn.sigmoid(logits)
    part_real, part_imag = band_part(mask_map, cos_rows, sin_rows, cos_full, sin_full)
    spec_real, spec_imag = lax.psum((part_real, part_imag), "rows")
    spec_real = spec_real / full_len
    spec_imag = spec_imag / full_len
    filt_real, filt_imag = filter_all(kernels, spec_real, spec_imag)
    field_real, field_imag = synthesize(
        filt_real, filt_imag, cos_rows, sin_rows, cos_full, sin_full
    )
    local_power = jnp.sum(
        kernel_weights[:, None, None] * (field_real * field_real + field_imag * field_imag), axis=0
    )
    intensity = lax.psum(local_power, "kern")
    grad_intensity = resist_grad(intensity, target)
    factor = 2.0 * kernel_weights[:, None, None] * grad_intensity[None]
    dy_real, dy_imag = analyze(
        factor * field_real, factor * field_imag, cos_rows, sin_rows, cos_full, sin_full
    )
    dy_real, dy_imag = lax.psum((dy_real, dy_imag), "rows")
    local_real, local_imag = conj_combine(kernels, dy_real, dy_imag)
    grad_real, grad_imag = lax.psum((local_real, local_imag), "kern")
    grad_logits = back_rows(grad_real, grad_imag, cos_rows, sin_rows, cos_full, sin_full, mask_map)
    return (head_weight[:, None, None] * grad_logits[None]).astype(jnp.bfloat16)


def solution(mesh):
    return jax.shard_map(
        on_device,
        mesh=mesh,
        in_specs=(
            P("kern", ("clips", "rows"), None),
            P("kern"),
            P("kern", None, None, None),
            P("kern"),
            P(("clips", "rows"), None),
        ),
        out_specs=P("kern", ("clips", "rows"), None),
        check_vma=False,
    )
```

profile of v0, /device:TPU:0, one launch (start us, length us, event | category | flops | bytes accessed | tf_op | source)
XLA Modules:
  0.0 208.3 jit_solution(7426696078790308123)
XLA Ops:
  6.5 0.6 copy-done.4
  7.2 1.0 multiply_reduce_fusion
  8.2 3.7 %psum.56 = f32[32,256]{1,0:T(8,128)S(1)} all-reduce(f32[32,256]{1,0:T(8,128)S(1)} %multiply_reduce_fusion), channel_id=1, replica_groups=mesh['clips'=2,'rows'=8,'kern'=2] {'kern'}, use_global_device_ids=true, to_apply=%region_1.2 | all-reduce | flops 8192 | bytes 65536 | tf_op jit(solution)/shard_map/psum | solution.py:125
  11.9 0.7 convolution_negate_fusion
  12.6 0.7 fusion.36
  14.0 1.0 fusion.7
  15.0 1.0 fusion.6
  16.0 0.6 copy-done.5
  17.1 71.3 %all-reduce.9.cloned.1.call-done = (f32[128,128]{0,1:T(8,128)}, f32[128,128]{0,1:T(8,128)}) async-done(((f32[128,128]{0,1:T(8,128)}, f32[128,128]{0,1:T(8,128)}), (f32[128,128]{0,1:T(8,128)}, f32[128,128]{0,1:T(8,128)})) %all-reduce.9.cloned.1.call-update) | async-done | bytes 131088 | tf_op jit(solution)/shard_map/psum | solution.py:128
  88.4 0.9 broadcast_multiply_fusion
  89.3 0.5 fusion.45
  90.9 0.8 fusion.41
  91.6 0.8 fusion.34
  92.9 0.8 fusion.4
  93.7 0.8 multiply_add_fusion
  94.5 3.6 %psum.59 = f32[32,256]{1,0:T(8,128)S(1)} all-reduce(f32[32,256]{1,0:T(8,128)S(1)} %multiply_reduce_fusion.1), channel_id=1, replica_groups=mesh['clips'=2,'rows'=8,'kern'=2] {'kern'}, use_global_device_ids=true, to_apply=%region_5.6 | all-reduce | flops 8192 | bytes 65536 | tf_op jit(solution)/shard_map/psum | solution.py:138
  98.3 0.8 fusion.29
  99.1 0.8 fusion.31
  99.8 0.8 convolution_subtract_fusion.2
  100.6 0.8 convolution_add_fusion.2
  101.4 0.6 fusion.58
  102.0 0.6 fusion.60
  102.7 1.4 fusion.1
  104.0 1.3 fusion.3
  105.5 71.9 %all-reduce.7.cloned.1.call-done = (f32[4,128,128]{1,2,0:T(8,128)}, f32[4,128,128]{1,2,0:T(8,128)}) async-done(((f32[4,128,128]{1,2,0:T(8,128)}, f32[4,128,128]{1,2,0:T(8,128)}), (f32[4,128,128]{1,2,0:T(8,128)}, f32[4,128,128]{1,2,0:T(8,128)})) %all-reduce.7.cloned.1.call-update) | async-done | bytes 524304 | tf_op jit(solution)/shard_map/psum | solution.py:144
  177.4 1.8 fusion.16
  179.1 17.8 %all-reduce.11.cloned.1.call-done = (f32[128,128]{0,1:T(8,128)}, f32[128,128]{0,1:T(8,128)}) async-done(((f32[128,128]{0,1:T(8,128)}, f32[128,128]{0,1:T(8,128)}), (f32[128,128]{0,1:T(8,128)}, f32[128,128]{0,1:T(8,128)})) %all-reduce.11.cloned.1.call-update) | async-done | bytes 131088 | tf_op jit(solution)/shard_map/psum | solution.py:146
  196.9 1.2 fusion.69
  198.7 0.5 copy-done.1
  199.6 0.7 fusion.27
  200.3 0.7 fusion.10
  201.1 0.7 multiply_convert_fusion
  (34 shorter events, 3.9 us)
Async XLA Ops:
  6.5 81.9 %all-reduce.9.cloned.1.call-start = ((), (), s32[]{:S(2)}) async-start(), calls=%async_computation.1 | async-start | bytes 262144 | tf_op jit(solution)/shard_map/psum | solution.py:128
  6.5 0.7 copy-start.4
  12.6 4.2 %copy-start = (f32[4,2,128,128]{3,2,1,0:T(8,128)S(1)}, f32[4,2,128,128]{3,2,1,0:T(8,128)}, u32[]{:S(2)}) copy-start(f32[4,2,128,128]{3,2,1,0:T(8,128)} %param.7) | copy-start | bytes 1572868
  15.9 0.7 copy-start.5
  16.0 161.4 %all-reduce.7.cloned.1.call-start = ((), (), s32[]{:S(2)}) async-start(), calls=%async_computation | async-start | bytes 1048576 | tf_op jit(solution)/shard_map/psum | solution.py:144
  94.5 3.6 %copy-start.3 = (bf16[32,256]{1,0:T(8,128)(2,1)S(1)}, bf16[32,256]{1,0:T(8,128)(2,1)}, u32[]{:S(2)}) copy-start(bf16[32,256]{1,0:T(8,128)(2,1)} %param.9) | copy-start | bytes 49156
  105.4 91.5 %all-reduce.11.cloned.1.call-start = ((), (), s32[]{:S(2)}) async-start(), calls=%async_computation.2 | async-start | bytes 262144 | tf_op jit(solution)/shard_map/psum | solution.py:146
  196.9 1.2 copy-start.2
  198.4 0.9 copy-start.1
Sparse Core Ops, SparseCore 0:
  16.1 72.2 all-reduce.8
  105.5 71.7 all-reduce.6
  179.7 17.1 all-reduce.10
where the time goes:
time: 209 us; the launch traced here: 208 us
  waiting for transfers between devices  161 us (77%)
  matrix products  19.6 us (9%)
  between operations  13.4 us (6%)
  blocking collectives  7.27 us (3%)
  other arithmetic  4.57 us (2%)
  local copies, waits for them, and re-layouts  2.28 us (1%)
    psum x1, waiting for transfers between devices, on_device(): dy_real, dy_imag = lax.psum((dy_real, dy_imag), 'rows')  71.9 us
    psum x1, waiting for transfers between devices, on_device(): spec_real, spec_imag = lax.psum((part_real, part_imag), 'rows')  71.3 us
    psum x1, waiting for transfers between devices, on_device(): grad_real, grad_imag = lax.psum((local_real, local_imag), 'kern')  17.8 us
    dot_general x8, matrix products, batch_left(): jnp.einsum('rs,krt->kst', lookup, blocks, precision=precise, preferred_el...  6.59 us
    dot_general x10, matrix products, right_prod(): jnp.dot(lhs_part, lookup, precision=precise, preferred_element_type=jnp.f...  6.49 us
    dot_general x6, matrix products, right_trans(): lax.dot_general(lhs_part, lookup, (((1,), (1,)), ((), ())), precision=pre...  4.52 us
  transfers between devices with their start and end apart: 3, of which 3 were waited for; matrix products, arithmetic and copies ran while one was open for 0% of the time, Pallas kernels for 0%

commit v1 on v0

--- a/solution.py
+++ b/solution.py
@@ -1,8 +1,13 @@
+import functools
 import math
 
 import jax
 import jax.numpy as jnp
+import ml_dtypes
+import numpy as np
 from jax import lax
+from jax.experimental import pallas as pl
+from jax.experimental.pallas import tpu as pltpu
 from jax.sharding import PartitionSpec as P
 
 precise = lax.Precision.HIGHEST
@@ -148,9 +153,310 @@
     return (head_weight[:, None, None] * grad_logits[None]).astype(jnp.bfloat16)
 
 
+MESH = pl.DeviceIdType.MESH
+f32 = jnp.float32
+bf16 = jnp.bfloat16
+
+
+def halves(table):
+    high = table.astype(np.float32).astype(ml_dtypes.bfloat16)
+    low = (table - high.astype(np.float64)).astype(np.float32).astype(ml_dtypes.bfloat16)
+    return high, low
+
+
+def make_tables(full_len, band_len, row_count, chips):
+    frequency = np.arange(band_len) - band_len // 2
+    phases = (np.arange(full_len)[:, None] * frequency[None, :]) % full_len
+    angles = phases * (2.0 * math.pi / full_len)
+    cos, sin = np.cos(angles), np.sin(angles)
+    half = row_count // 2
+    rf = np.block([[cos.T, sin.T], [-sin.T, cos.T]])
+    rq = rf.reshape(2 * band_len, 2, chips, row_count).transpose(0, 2, 1, 3).reshape(rf.shape)
+    by_core = lambda t: t.reshape(chips, 2, half, band_len)
+    lt, lq, ld = [], [], []
+    for core in range(2):
+        c = by_core(cos)[:, core].reshape(-1, band_len)
+        s = by_core(sin)[:, core].reshape(-1, band_len)
+        lt.append(np.stack(halves(np.block([[c.T, s.T], [-s.T, c.T]]))))
+    for chip in range(chips):
+        for core in range(2):
+            c, s = by_core(cos)[chip, core], by_core(sin)[chip, core]
+            high, low = halves(np.block([[c, -s], [s, c]]))
+            lq.append(np.concatenate([high, low], axis=0))
+            ld.append(np.concatenate([high.T, low.T, high.T], axis=1))
+    return (
+        np.stack(halves(rf)),
+        np.stack(halves(rf.T)),
+        np.stack(halves(rq)),
+        np.stack(lt),
+        np.stack(lq),
+        np.stack(ld),
+    )
+
+
+def split(x):
+    high = x.astype(bf16)
+    return high, (x - high.astype(f32)).astype(bf16)
+
+
+def mm(a, b):
+    return jnp.dot(a, b, preferred_element_type=f32)
+
+
+def dot3(a, b_high, b_low):
+    high, low = split(a)
+    rows = a.shape[0]
+    both = mm(jnp.concatenate([high, low], axis=0), b_high)
+    return both[:rows] + both[rows:] + mm(high, b_low)
+
+
+def fused(
+    hw, kw, feat, tgt, ker_hbm, rf_hbm, rb_hbm, rq_hbm, lt_hbm, lq_hbm, ld_hbm,
+    out,
+    ker, rf, rb, rq, lt, lq, ld,
+    logit_send, logit_recv, wts, hbuf, x_send, x_recv, gs, gbuf, ps, pbuf, pt, mask_buf,
+    local_sem, pair_send, pair_recv, h_send_sem, h_recv_sem, g_send_sem, g_recv_sem, p_send_sem, p_recv_sem,
+):
+    chips, half, _ = hbuf.shape
+    band = ker.shape[-1]
+    full = feat.shape[-1]
+    channels = feat.shape[0]
+    kpc = ker.shape[1]
+    kcount = 2 * kpc
+    n = 2 * chips
+    r = lax.axis_index("rows")
+    c = lax.axis_index("kern")
+    me = 2 * r + c
+    partner = {"rows": r, "kern": 1 - c}
+
+    def peer(d):
+        p = lax.rem(me + d, n)
+        return p, {"rows": p // 2, "kern": lax.rem(p, 2)}
+
+    barrier = pltpu.get_barrier_semaphore()
+    for d in range(1, n):
+        pl.semaphore_signal(barrier, inc=1, device_id=peer(d)[1], device_id_type=MESH)
+
+    def local(src, dst, i):
+        copy = pltpu.make_async_copy(src, dst, local_sem.at[i])
+        copy.start()
+        return copy
+
+    get_rb = local(rb_hbm, rb, 0)
+    get_lt = local(lt_hbm.at[c], lt, 1)
+    get_ker = local(ker_hbm, ker.at[c], 2)
+    get_lq = local(lq_hbm.at[me], lq, 3)
+    get_rf = local(rf_hbm, rf, 4)
+    get_ld = local(ld_hbm.at[me], ld, 5)
+    get_rq = local(rq_hbm, rq, 6)
+
+    total = hw[0] * feat[0].astype(f32)
+    for ch in range(1, channels):
+        total = total + hw[ch] * feat[ch].astype(f32)
+    logit_send[...] = total
+    for k in range(kpc):
+        wts[c, k : k + 1, :] = jnp.full((1, wts.shape[-1]), kw[k], f32)
+
+    pl.semaphore_wait(barrier, n - 1)
+
+    def remote(src, dst, send, recv, device):
+        return pltpu.make_async_remote_copy(
+            src_ref=src, dst_ref=dst, send_sem=send, recv_sem=recv, device_id=device, device_id_type=MESH
+        )
+
+    def pair(src, dst, i):
+        return remote(src, dst, pair_send.at[i], pair_recv.at[i], partner)
+
+    swap_logits = pair(logit_send, logit_recv, 0)
+    swap_logits.start()
+    swap_kernels = pair(ker_hbm, ker.at[c], 1)
+    swap_weights = pair(wts.at[c], wts.at[c], 2)
+
+    swap_logits.wait_recv()
+    mask = jax.nn.sigmoid(logit_send[...] + logit_recv[...])
+    mask_buf[...] = mask
+    get_rb.wait()
+    mine = mask_buf[pl.ds(pl.multiple_of(half * c, half), half), :]
+    hbuf[r] = dot3(mine, rb[0, :full], rb[1, :full])
+    sends = []
+    for d in range(1, chips):
+        p = lax.rem(r + d, chips)
+        copy = remote(hbuf.at[r], hbuf.at[r], h_send_sem.at[d], h_recv_sem.at[r], {"rows": p, "kern": c})
+        copy.start()
+        sends.append(copy)
+    swap_weights.start()
+    swap_kernels.start()
+    get_lt.wait()
+    for d in range(1, chips):
+        p = lax.rem(r + d, chips)
+        remote(hbuf.at[p], hbuf.at[p], h_send_sem.at[d], h_recv_sem.at[p], {"rows": p, "kern": c}).wait_recv()
+    rows = hbuf[...].reshape(chips * half, 2 * band)
+    rh_high, rh_low = split(jnp.concatenate([rows[:, :band], rows[:, band:]], axis=0))
+    x_send[...] = mm(lt[0], rh_high) + (mm(lt[1], rh_high) + mm(lt[0], rh_low))
+    swap_x = pair(x_send, x_recv, 3)
+    swap_x.start()
+    get_ker.wait()
+    get_lq.wait()
+    pair(ker_hbm, ker.at[1 - c], 1).wait_recv()
+    pair(wts.at[1 - c], wts.at[1 - c], 2).wait_recv()
+    swap_x.wait_recv()
+    x = (x_send[...] + x_recv[...]) * (1.0 / (full * band))
+    xr, xi = x[:band], x[band:]
+
+    kernel_of = lambda k, part: ker[k // kpc, k % kpc, part]
+    weight_of = lambda k: wts[k // kpc, k % kpc : k % kpc + 1, :]
+    qs = []
+    for k0 in range(0, kcount, 2):
+        columns = []
+        for k in (k0, k0 + 1):
+            kr, ki = kernel_of(k, 0), kernel_of(k, 1)
+            columns.append(jnp.concatenate([kr * xr - ki * xi, kr * xi + ki * xr], axis=0))
+        f_high, f_low = split(jnp.concatenate(columns, axis=1))
+        both = mm(lq[...], f_high)
+        q = both[: 2 * half] + both[2 * half :] + mm(lq[: 2 * half], f_low)
+        for j in range(2):
+            part = q[:, j * band : (j + 1) * band]
+            qs.append(jnp.concatenate([part[:half], part[half:]], axis=1))
+    get_rf.wait()
+    field = dot3(jnp.concatenate(qs, axis=0), rf[0], rf[1])
+
+    power = jnp.zeros((half, full), f32)
+    for k in range(kcount):
+        fr = field[k * half : (k + 1) * half, :full]
+        fi = field[k * half : (k + 1) * half, full:]
+        w = jnp.concatenate([weight_of(k)] * (full // wts.shape[-1]), axis=1)
+        power = power + w * (fr * fr + fi * fi)
+    target = tgt[pl.ds(pl.multiple_of(half * c, half), half), :].astype(f32)
+    resist = jax.nn.sigmoid(steepness * (power - threshold))
+    grad_power = 2.0 * (resist - target) * steepness * resist * (1.0 - resist)
+    grads = []
+    for k in range(kcount):
+        w = jnp.concatenate([weight_of(k)] * (full // wts.shape[-1]), axis=1)
+        factor = 2.0 * w * grad_power
+        grads.append(jnp.concatenate([factor, factor], axis=1) * field[k * half : (k + 1) * half])
+    b = dot3(jnp.concatenate(grads, axis=0), rb[0], rb[1])
+
+    get_ld.wait()
+    gr = jnp.zeros((band, band), f32)
+    gi = jnp.zeros((band, band), f32)
+    for k0 in range(0, kcount, 2):
+        columns = []
+        for k in (k0, k0 + 1):
+            part = b[k * half : (k + 1) * half]
+            columns.append(jnp.concatenate([part[:, :band], part[:, band:]], axis=0))
+        b_high, b_low = split(jnp.concatenate(columns, axis=1))
+        dy = mm(ld[...], jnp.concatenate([b_high, b_high, b_low], axis=0))
+        for j, k in enumerate((k0, k0 + 1)):
+            dr, di = dy[:band, j * band : (j + 1) * band], dy[band:, j * band : (j + 1) * band]
+            kr, ki = kernel_of(k, 0), kernel_of(k, 1)
+            gr = gr + (kr * dr + ki * di)
+            gi = gi + (kr * di - ki * dr)
+    gs[:, 0] = gr.T.reshape(n, band // n, band)
+    gs[:, 1] = gi.T.reshape(n, band // n, band)
+
+    for d in range(1, n):
+        p, device = peer(d)
+        copy = remote(gs.at[p], gbuf.at[d], g_send_sem.at[d], g_recv_sem.at[d], device)
+        copy.start()
+        sends.append(copy)
+    get_rq.wait()
+    mask = mask_buf[...]
+    slope = mask * (1.0 - mask) * (1.0 / (full * band))
+    g = gs[me]
+    for d in range(1, n):
+        remote(gs.at[0], gbuf.at[d], g_send_sem.at[d], g_recv_sem.at[d], peer(d)[1]).wait_recv()
+        g = g + gbuf[d]
+    q = dot3(jnp.concatenate([g[0], g[1]], axis=1), rq[0], rq[1])
+    tiles = chips // 2
+    for j in range(tiles):
+        ps[j] = q[:, 128 * j : 128 * (j + 1)]
+    pbuf[me] = ps[r // 2]
+    for d in range(1, n):
+        p, device = peer(d)
+        copy = remote(ps.at[p // 4], pbuf.at[me], p_send_sem.at[d], p_recv_sem.at[me], device)
+        copy.start()
+        sends.append(copy)
+    for d in range(1, n):
+        p, device = peer(d)
+        remote(ps.at[0], pbuf.at[p], p_send_sem.at[d], p_recv_sem.at[p], device).wait_recv()
+    pt[...] = pbuf[...].reshape(band, 128).T
+    base = pl.multiple_of(4 * half * lax.rem(r, 2), 4 * half)
+    lhs = jnp.concatenate([pt[pl.ds(base, 2 * half), :], pt[pl.ds(base + 2 * half, 2 * half), :]], axis=1)
+    grad_mask = dot3(lhs, rf[0, :, :full], rf[1, :, :full])
+    out[...] = grad_mask * slope
+
+    for copy in (swap_logits, swap_kernels, swap_weights, swap_x, *sends):
+        copy.wait_send()
+
+
+def fused_on_device(tables, chips, features, head_weight, kernels, kernel_weights, target):
+    channels, row_count, full = features.shape
+    kpc, _, band, _ = kernels.shape
+    half = row_count // 2
+    n = 2 * chips
+    vmem = pl.BlockSpec(memory_space=pltpu.VMEM)
+    smem = pl.BlockSpec(memory_space=pltpu.SMEM)
+    anywhere = pl.BlockSpec(memory_space=pl.ANY)
+    dma = pltpu.SemaphoreType.DMA
+    rf, rb, rq, lt, lq, ld = tables
+    grad_logits = pl.pallas_call(
+        fused,
+        out_shape=jax.ShapeDtypeStruct((row_count, full), f32),
+        in_specs=[smem, smem, vmem, vmem] + [anywhere] * 7,
+        out_specs=vmem,
+        scratch_shapes=[
+            pltpu.VMEM((2, kpc, 2, band, band), f32),
+            pltpu.VMEM(rf.shape, bf16),
+            pltpu.VMEM(rb.shape, bf16),
+            pltpu.VMEM(rq.shape, bf16),
+            pltpu.VMEM(lt.shape[1:], bf16),
+            pltpu.VMEM(lq.shape[1:], bf16),
+            pltpu.VMEM(ld.shape[1:], bf16),
+            pltpu.VMEM((row_count, full), f32),
+            pltpu.VMEM((row_count, full), f32),
+            pltpu.VMEM((2, 8, 128), f32),
+            pltpu.VMEM((chips, half, 2 * band), f32),
+            pltpu.VMEM((2 * band, band), f32),
+            pltpu.VMEM((2 * band, band), f32),
+            pltpu.VMEM((n, 2, band // n, band), f32),
+            pltpu.VMEM((n, 2, band // n, band), f32),
+            pltpu.VMEM((chips // 2, band // n, 128), f32),
+            pltpu.VMEM((n, band // n, 128), f32),
+            pltpu.VMEM((128, band), f32),
+            pltpu.VMEM((row_count, full), f32),
+            dma((7,)),
+            dma((4,)),
+            dma((4,)),
+            dma((chips,)),
+            dma((chips,)),
+            dma((n,)),
+            dma((n,)),
+            dma((n,)),
+            dma((n,)),
+        ],
+        compiler_params=pltpu.CompilerParams(
+            collective_id=0, has_side_effects=True, vmem_limit_bytes=32 * 1024 * 1024
+        ),
+    )(head_weight, kernel_weights, features, target, kernels, *[jnp.asarray(t) for t in (rf, rb, rq, lt, lq, ld)])
+    return (head_weight[:, None, None] * grad_logits[None]).astype(jnp.bfloat16)
+
+
+def choose(mesh, features, head_weight, kernels, kernel_weights, target):
+    row_count, full = target.shape
+    channels, kpc, band = features.shape[0], kernels.shape[0], kernels.shape[-1]
+    chips = mesh.shape["rows"]
+    fits = (
+        mesh.shape["kern"] == 2 and row_count == 32 and chips == 8 and full == 256 and band == 128 and kpc == 4
+    )
+    if not fits:
+        return on_device(features, head_weight, kernels, kernel_weights, target)
+    tables = make_tables(full, band, row_count, chips)
+    return fused_on_device(tables, chips, features, head_weight, kernels, kernel_weights, target)
+
+
 def solution(mesh):
     return jax.shard_map(
-        on_device,
+        functools.partial(choose, mesh),
         mesh=mesh,
         in_specs=(
             P("kern", ("clips", "rows"), None),

time: 209 us -> 37.3 us (0.18)
  waiting for transfers between devices: 161 us -> 0 us
  Pallas kernels: 0 us -> 25.6 us
  matrix products: 19.6 us -> 0 us
  between operations: 13.4 us -> 0.02 us
  local copies, waits for them, and re-layouts: 2.28 us -> 10.4 us
  blocking collectives: 7.27 us -> 0 us
  other arithmetic: 4.57 us -> 0.74 us
    psum x3 -> x0, waiting for transfers between devices: 161 us -> none  [the longest x1 71.9 us: on_device(): dy_real, dy_imag = lax.psum((dy_real, dy_imag), 'rows')]
    pallas_call x0 -> x1, Pallas kernels: none -> 25.6 us  [fused_on_device(): pl.pallas_call(fused, out_shape=jax.ShapeDtypeStruct((row_count, full), f...]
    dot_general x28 -> x0, matrix products: 19.6 us -> none  [the longest x8 6.59 us: batch_left(): jnp.einsum('rs,krt->kst', lookup, blocks, precision=precise, preferred_el...]
    unnamed x14 -> x22, local copies, waits for them, and re-layouts: 2.08 us -> 10.4 us
    psum x2 -> x0, blocking collectives: 7.27 us -> none  [the longest x1 3.69 us: on_device(): logits = lax.psum(local_logits, 'kern')]
    reduce_sum x3 -> x0, other arithmetic: 2.83 us -> none  [the longest x1 1.75 us: conj_combine(): dx_imag = jnp.sum(gain_real * dy_imag - gain_imag * dy_real, axis=0)]
  transfers between devices with their start and end apart: 3 -> 0, of which waited for: 3 -> 0; matrix products, arithmetic and copies ran while one was open for 0% -> 0% of each run, Pallas kernels for 0% -> 0%
where the time goes in v1:
time: 37.3 us; the launch traced here: 36.8 us
  Pallas kernels  25.6 us (69%)
  local copies, waits for them, and re-layouts  10.4 us (28%)
  other arithmetic  0.74 us (2%)
    pallas_call x1, Pallas kernels, fused_on_device(): pl.pallas_call(fused, out_shape=jax.ShapeDtypeStruct((row_count, full), f...  25.6 us
    unnamed x22, local copies, waits for them, and re-layouts  10.4 us

profile of v1, /device:TPU:0, one launch (start us, length us, event | category | flops | bytes accessed | tf_op | source)
XLA Modules:
  0.0 36.8 jit_solution(16591532199780789680)
XLA Ops:
  0.0 0.0 copy-start
  0.0 1.2 %copy-done = bf16[16,256,96]{2,1,0:T(8,128)(2,1)S(1)} copy-done((bf16[16,256,96]{2,1,0:T(8,128)(2,1)S(1)}, bf16[16,256,96]{2,1,0:T(8,128)(2,1)}, u32[]{:S(2)}) %copy-start) | copy-done | bytes 786456
  1.2 0.0 copy-start.1
  1.2 1.0 %copy-done.1 = f32[4,2,128,128]{3,2,1,0:T(8,128)S(1)} copy-done((f32[4,2,128,128]{3,2,1,0:T(8,128)S(1)}, f32[4,2,128,128]{3,2,1,0:T(8,128)}, u32[]{:S(2)}) %copy-start.1) | copy-done | bytes 524312
  2.3 0.0 copy-start.2
  2.3 1.0 %copy-done.2 = bf16[16,64,256]{2,1,0:T(8,128)(2,1)S(1)} copy-done((bf16[16,64,256]{2,1,0:T(8,128)(2,1)S(1)}, bf16[16,64,256]{2,1,0:T(8,128)(2,1)}, u32[]{:S(2)}) %copy-start.2) | copy-done | bytes 524312
  3.3 0.0 copy-start.3
  3.3 1.0 %copy-done.3 = bf16[2,2,256,256]{3,2,1,0:T(8,128)(2,1)S(1)} copy-done((bf16[2,2,256,256]{3,2,1,0:T(8,128)(2,1)S(1)}, bf16[2,2,256,256]{3,2,1,0:T(8,128)(2,1)}, u32[]{:S(2)}) %copy-start.3) | copy-done | bytes 524312
  4.4 0.0 copy-start.4
  4.4 1.0 %copy-done.4 = bf16[2,256,512]{2,1,0:T(8,128)(2,1)S(1)} copy-done((bf16[2,256,512]{2,1,0:T(8,128)(2,1)S(1)}, bf16[2,256,512]{2,1,0:T(8,128)(2,1)}, u32[]{:S(2)}) %copy-start.4) | copy-done | bytes 524312
  5.4 0.0 copy-start.5
  5.4 1.0 %copy-done.5 = bf16[2,512,256]{2,1,0:T(8,128)(2,1)S(1)} copy-done((bf16[2,512,256]{2,1,0:T(8,128)(2,1)S(1)}, bf16[2,512,256]{2,1,0:T(8,128)(2,1)}, u32[]{:S(2)}) %copy-start.5) | copy-done | bytes 524312
  6.4 0.0 copy-start.6
  6.4 1.0 %copy-done.6 = bf16[2,256,512]{2,1,0:T(8,128)(2,1)S(1)} copy-done((bf16[2,256,512]{2,1,0:T(8,128)(2,1)S(1)}, bf16[2,256,512]{2,1,0:T(8,128)(2,1)}, u32[]{:S(2)}) %copy-start.6) | copy-done | bytes 524312
  7.5 0.0 copy-start.7
  7.5 0.9 %copy-done.7 = bf16[8,32,256]{2,1,0:T(8,128)(2,1)S(1)} copy-done((bf16[8,32,256]{2,1,0:T(8,128)(2,1)S(1)}, bf16[8,32,256]{2,1,0:T(8,128)(2,1)}, u32[]{:S(2)}) %copy-start.7) | copy-done | bytes 131096
  8.4 0.0 copy-start.8
  8.4 0.7 %copy-done.8 = bf16[32,256]{1,0:T(8,128)(2,1)S(1)} copy-done((bf16[32,256]{1,0:T(8,128)(2,1)S(1)}, bf16[32,256]{1,0:T(8,128)(2,1)}, u32[]{:S(2)}) %copy-start.8) | copy-done | bytes 16408
  9.1 0.0 copy-start.9
  9.1 0.7 %copy-done.9 = f32[8]{0:T(128)S(1)} copy-done((f32[8]{0:T(128)S(1)}, f32[8]{0:T(128)}, u32[]{:S(2)}) %copy-start.9) | copy-done | bytes 56
  9.8 0.0 copy-start.10
  9.8 0.7 %copy-done.10 = f32[4]{0:T(128)S(1)} copy-done((f32[4]{0:T(128)S(1)}, f32[4]{0:T(128)}, u32[]{:S(2)}) %copy-start.10) | copy-done | bytes 40
  10.4 25.6 %shard_map.109 = f32[32,256]{1,0:T(8,128)S(1)} custom-call(f32[8]{0:T(128)S(1)} %copy-done.9, f32[4]{0:T(128)S(1)} %copy-done.10, bf16[8,32,256]{2,1,0:T(8,128)(2,1)S(1)} %copy-done.7, bf16[32,256]{1,0:T(8,128)(2,1)S(1)} %copy-done.8, f32[4,2,128,128]{3,2,1,0:T(8,128)S(1)} %copy-done.1, bf16[2,256,512]{2,1,0:T(8,128)(2,1)S(1)} %copy-done.6, ...), custom_call_target="tpu_custom_call" | custom-call | tf_op jit(solution)/shard_map/pallas_call | solution.py:402
  36.0 0.7 %multiply_convert_fusion = bf16[8,32,256]{2,1,0:T(8,128)(2,1)} fusion(f32[32,256]{1,0:T(8,128)S(1)} %shard_map.109, f32[8]{0:T(128)S(1)} %copy-done.9), kind=kLoop, calls=%fused_computation | loop fusion | flops 131072 | bytes 163872 | tf_op jit(solution)/shard_map/convert_element_type | solution.py:441
Async XLA Ops:
  0.0 1.2 %copy-start = (bf16[16,256,96]{2,1,0:T(8,128)(2,1)S(1)}, bf16[16,256,96]{2,1,0:T(8,128)(2,1)}, u32[]{:S(2)}) copy-start(bf16[16,256,96]{2,1,0:T(8,128)(2,1)} %constant.17.clone.ld_hbm) | copy-start | bytes 2359300
  1.2 1.0 %copy-start.1 = (f32[4,2,128,128]{3,2,1,0:T(8,128)S(1)}, f32[4,2,128,128]{3,2,1,0:T(8,128)}, u32[]{:S(2)}) copy-start(f32[4,2,128,128]{3,2,1,0:T(8,128)} %ker_hbm.1) | copy-start | bytes 1572868
  2.3 1.0 %copy-start.2 = (bf16[16,64,256]{2,1,0:T(8,128)(2,1)S(1)}, bf16[16,64,256]{2,1,0:T(8,128)(2,1)}, u32[]{:S(2)}) copy-start(bf16[16,64,256]{2,1,0:T(8,128)(2,1)} %constant.16.clone.lq_hbm) | copy-start | bytes 1572868
  3.3 1.0 %copy-start.3 = (bf16[2,2,256,256]{3,2,1,0:T(8,128)(2,1)S(1)}, bf16[2,2,256,256]{3,2,1,0:T(8,128)(2,1)}, u32[]{:S(2)}) copy-start(bf16[2,2,256,256]{3,2,1,0:T(8,128)(2,1)} %constant.15.clone.lt_hbm) | copy-start | bytes 1572868
  4.4 1.0 %copy-start.4 = (bf16[2,256,512]{2,1,0:T(8,128)(2,1)S(1)}, bf16[2,256,512]{2,1,0:T(8,128)(2,1)}, u32[]{:S(2)}) copy-start(bf16[2,256,512]{2,1,0:T(8,128)(2,1)} %constant.14.clone.rq_hbm) | copy-start | bytes 1572868
  5.4 1.0 %copy-start.5 = (bf16[2,512,256]{2,1,0:T(8,128)(2,1)S(1)}, bf16[2,512,256]{2,1,0:T(8,128)(2,1)}, u32[]{:S(2)}) copy-start(bf16[2,512,256]{2,1,0:T(8,128)(2,1)} %constant.13.clone.rb_hbm) | copy-start | bytes 1572868
  6.4 1.0 %copy-start.6 = (bf16[2,256,512]{2,1,0:T(8,128)(2,1)S(1)}, bf16[2,256,512]{2,1,0:T(8,128)(2,1)}, u32[]{:S(2)}) copy-start(bf16[2,256,512]{2,1,0:T(8,128)(2,1)} %constant.12.clone.rf_hbm) | copy-start | bytes 1572868
  7.5 0.9 %copy-start.7 = (bf16[8,32,256]{2,1,0:T(8,128)(2,1)S(1)}, bf16[8,32,256]{2,1,0:T(8,128)(2,1)}, u32[]{:S(2)}) copy-start(bf16[8,32,256]{2,1,0:T(8,128)(2,1)} %feat.1) | copy-start | bytes 393220
  8.4 0.7 %copy-start.8 = (bf16[32,256]{1,0:T(8,128)(2,1)S(1)}, bf16[32,256]{1,0:T(8,128)(2,1)}, u32[]{:S(2)}) copy-start(bf16[32,256]{1,0:T(8,128)(2,1)} %tgt.1) | copy-start | bytes 49156
  9.1 0.7 %copy-start.9 = (f32[8]{0:T(128)S(1)}, f32[8]{0:T(128)}, u32[]{:S(2)}) copy-start(f32[8]{0:T(128)} %hw.1) | copy-start | bytes 100
  9.8 0.7 %copy-start.10 = (f32[4]{0:T(128)S(1)}, f32[4]{0:T(128)}, u32[]{:S(2)}) copy-start(f32[4]{0:T(128)} %kw.1) | copy-start | bytes 52

commit v2 on v1

--- a/solution.py
+++ b/solution.py
@@ -154,6 +154,7 @@
 
 
 MESH = pl.DeviceIdType.MESH
+VMEM_BYTES = 63 * 1024 * 1024
 f32 = jnp.float32
 bf16 = jnp.bfloat16
 
@@ -173,10 +174,12 @@
     rf = np.block([[cos.T, sin.T], [-sin.T, cos.T]])
     rq = rf.reshape(2 * band_len, 2, chips, row_count).transpose(0, 2, 1, 3).reshape(rf.shape)
     by_core = lambda t: t.reshape(chips, 2, half, band_len)
-    lt, lq, ld = [], [], []
+    lt, lq, ld, gt = [], [], [], []
     for core in range(2):
         c = by_core(cos)[:, core].reshape(-1, band_len)
         s = by_core(sin)[:, core].reshape(-1, band_len)
+        mine = slice(core * band_len // 2, (core + 1) * band_len // 2)
+        gt.append(np.stack(halves(np.concatenate([cos.T[mine], -sin.T[mine]], axis=0))))
         lt.append(np.stack(halves(np.block([[c.T, s.T], [-s.T, c.T]]))))
     for chip in range(chips):
         for core in range(2):
@@ -191,6 +194,7 @@
         np.stack(lt),
         np.stack(lq),
         np.stack(ld),
+        np.stack(gt),
     )
 
 
@@ -211,10 +215,10 @@
 
 
 def fused(
-    hw, kw, feat, tgt, ker_hbm, rf_hbm, rb_hbm, rq_hbm, lt_hbm, lq_hbm, ld_hbm,
+    hw_hbm, kw_hbm, feat_hbm, tgt_hbm, ker_hbm, rf_hbm, rb_hbm, rq_hbm, lt_hbm, lq_hbm, ld_hbm, gt_hbm,
     out,
-    ker, rf, rb, rq, lt, lq, ld,
-    logit_send, logit_recv, wts, hbuf, x_send, x_recv, gs, gbuf, ps, pbuf, pt, mask_buf,
+    hw, kw, feat, tgt, ker, rf, rb, rq, lt, lq, ld, gt,
+    logit_send, logit_recv, wts, hbuf, x_send, x_recv, gs, g_pair, g_sum, gbuf, ps, pbuf, pt, gm_send, gm_recv, mask_buf,
     local_sem, pair_send, pair_recv, h_send_sem, h_recv_sem, g_send_sem, g_recv_sem, p_send_sem, p_recv_sem,
 ):
     chips, half, _ = hbuf.shape
@@ -229,19 +233,28 @@
     me = 2 * r + c
     partner = {"rows": r, "kern": 1 - c}
 
-    def peer(d):
-        p = lax.rem(me + d, n)
-        return p, {"rows": p // 2, "kern": lax.rem(p, 2)}
-
     barrier = pltpu.get_barrier_semaphore()
-    for d in range(1, n):
-        pl.semaphore_signal(barrier, inc=1, device_id=peer(d)[1], device_id_type=MESH)
+    for d in range(1, chips):
+        other = {"rows": lax.rem(r + d, chips), "kern": c}
+        pl.semaphore_signal(barrier, inc=1, device_id=other, device_id_type=MESH)
+    pl.semaphore_signal(barrier, inc=1, device_id=partner, device_id_type=MESH)
+
+    pending = []
+
+    def need(wait):
+        wait()
+        pending.remove(wait)
 
     def local(src, dst, i):
         copy = pltpu.make_async_copy(src, dst, local_sem.at[i])
         copy.start()
-        return copy
-
+        pending.append(copy.wait)
+        return pending[-1]
+
+    get_hw = local(hw_hbm, hw, 7)
+    get_feat = local(feat_hbm, feat, 8)
+    get_kw = local(kw_hbm, kw, 9)
+    get_tgt = local(tgt_hbm, tgt, 10)
     get_rb = local(rb_hbm, rb, 0)
     get_lt = local(lt_hbm.at[c], lt, 1)
     get_ker = local(ker_hbm, ker.at[c], 2)
@@ -249,44 +262,53 @@
     get_rf = local(rf_hbm, rf, 4)
     get_ld = local(ld_hbm.at[me], ld, 5)
     get_rq = local(rq_hbm, rq, 6)
-
+    get_gt = local(gt_hbm.at[c], gt, 11)
+
+    need(get_hw)
+    need(get_feat)
     total = hw[0] * feat[0].astype(f32)
     for ch in range(1, channels):
         total = total + hw[ch] * feat[ch].astype(f32)
     logit_send[...] = total
+    need(get_kw)
     for k in range(kpc):
         wts[c, k : k + 1, :] = jnp.full((1, wts.shape[-1]), kw[k], f32)
 
-    pl.semaphore_wait(barrier, n - 1)
+    pl.semaphore_wait(barrier, chips)
 
     def remote(src, dst, send, recv, device):
         return pltpu.make_async_remote_copy(
             src_ref=src, dst_ref=dst, send_sem=send, recv_sem=recv, device_id=device, device_id_type=MESH
         )
 
+    def send(copy):
+        copy.start()
+        pending.append(copy.wait_send)
+
     def pair(src, dst, i):
         return remote(src, dst, pair_send.at[i], pair_recv.at[i], partner)
 
     swap_logits = pair(logit_send, logit_recv, 0)
-    swap_logits.start()
+    send(swap_logits)
     swap_kernels = pair(ker_hbm, ker.at[c], 1)
     swap_weights = pair(wts.at[c], wts.at[c], 2)
 
     swap_logits.wait_recv()
     mask = jax.nn.sigmoid(logit_send[...] + logit_recv[...])
     mask_buf[...] = mask
-    get_rb.wait()
+    need(get_rb)
     mine = mask_buf[pl.ds(pl.multiple_of(half * c, half), half), :]
     hbuf[r] = dot3(mine, rb[0, :full], rb[1, :full])
-    sends = []
     for d in range(1, chips):
         p = lax.rem(r + d, chips)
         copy = remote(hbuf.at[r], hbuf.at[r], h_send_sem.at[d], h_recv_sem.at[r], {"rows": p, "kern": c})
-        copy.start()
-        sends.append(copy)
-    swap_weights.start()
-    swap_kernels.start()
-    get_lt.wait()
+        send(copy)
+    send(swap_weights)
+    send(swap_kernels)
+    take_weights = pair(wts.at[1 - c], wts.at[1 - c], 2).wait_recv
+    take_kernels = pair(ker_hbm, ker.at[1 - c], 1).wait_recv
+    pending.extend((take_weights, take_kernels))
+    need(get_lt)
     for d in range(1, chips):
         p = lax.rem(r + d, chips)
         remote(hbuf.at[p], hbuf.at[p], h_send_sem.at[d], h_recv_sem.at[p], {"rows": p, "kern": c}).wait_recv()
@@ -294,11 +316,11 @@
     rh_high, rh_low = split(jnp.concatenate([rows[:, :band], rows[:, band:]], axis=0))
     x_send[...] = mm(lt[0], rh_high) + (mm(lt[1], rh_high) + mm(lt[0], rh_low))
     swap_x = pair(x_send, x_recv, 3)
-    swap_x.start()
-    get_ker.wait()
-    get_lq.wait()
-    pair(ker_hbm, ker.at[1 - c], 1).wait_recv()
-    pair(wts.at[1 - c], wts.at[1 - c], 2).wait_recv()
+    send(swap_x)
+    need(get_ker)
+    need(get_lq)
+    need(take_kernels)
+    need(take_weights)
     swap_x.wait_recv()
     x = (x_send[...] + x_recv[...]) * (1.0 / (full * band))
     xr, xi = x[:band], x[band:]
@@ -317,7 +339,7 @@
         for j in range(2):
             part = q[:, j * band : (j + 1) * band]
             qs.append(jnp.concatenate([part[:half], part[half:]], axis=1))
-    get_rf.wait()
+    need(get_rf)
     field = dot3(jnp.concatenate(qs, axis=0), rf[0], rf[1])
 
     power = jnp.zeros((half, full), f32)
@@ -326,6 +348,7 @@
         fi = field[k * half : (k + 1) * half, full:]
         w = jnp.concatenate([weight_of(k)] * (full // wts.shape[-1]), axis=1)
         power = power + w * (fr * fr + fi * fi)
+    need(get_tgt)
     target = tgt[pl.ds(pl.multiple_of(half * c, half), half), :].astype(f32)
     resist = jax.nn.sigmoid(steepness * (power - threshold))
     grad_power = 2.0 * (resist - target) * steepness * resist * (1.0 - resist)
@@ -336,7 +359,7 @@
         grads.append(jnp.concatenate([factor, factor], axis=1) * field[k * half : (k + 1) * half])
     b = dot3(jnp.concatenate(grads, axis=0), rb[0], rb[1])
 
-    get_ld.wait()
+    need(get_ld)
     gr = jnp.zeros((band, band), f32)
     gi = jnp.zeros((band, band), f32)
     for k0 in range(0, kcount, 2):
@@ -351,42 +374,44 @@
             kr, ki = kernel_of(k, 0), kernel_of(k, 1)
             gr = gr + (kr * dr + ki * di)
             gi = gi + (kr * di - ki * dr)
-    gs[:, 0] = gr.T.reshape(n, band // n, band)
-    gs[:, 1] = gi.T.reshape(n, band // n, band)
-
-    for d in range(1, n):
-        p, device = peer(d)
-        copy = remote(gs.at[p], gbuf.at[d], g_send_sem.at[d], g_recv_sem.at[d], device)
-        copy.start()
-        sends.append(copy)
-    get_rq.wait()
+    gs[:, :, 0] = gr.T.reshape(2, chips, band // n, band)
+    gs[:, :, 1] = gi.T.reshape(2, chips, band // n, band)
+    swap_g = pair(gs.at[1 - c], g_pair, 4)
+    send(swap_g)
+    need(get_rq)
+    need(get_gt)
     mask = mask_buf[...]
     slope = mask * (1.0 - mask) * (1.0 / (full * band))
-    g = gs[me]
-    for d in range(1, n):
-        remote(gs.at[0], gbuf.at[d], g_send_sem.at[d], g_recv_sem.at[d], peer(d)[1]).wait_recv()
+    swap_g.wait_recv()
+    g_sum[...] = gs[c] + g_pair[...]
+    for d in range(1, chips):
+        p = lax.rem(r + d, chips)
+        send(remote(g_sum.at[p], gbuf.at[d], g_send_sem.at[d], g_recv_sem.at[d], {"rows": p, "kern": c}))
+    g = g_sum[r]
+    for d in range(1, chips):
+        p = lax.rem(r + d, chips)
+        remote(g_sum.at[p], gbuf.at[d], g_send_sem.at[d], g_recv_sem.at[d], {"rows": p, "kern": c}).wait_recv()
         g = g + gbuf[d]
     q = dot3(jnp.concatenate([g[0], g[1]], axis=1), rq[0], rq[1])
-    tiles = chips // 2
-    for j in range(tiles):
+    for j in range(chips // 2):
         ps[j] = q[:, 128 * j : 128 * (j + 1)]
-    pbuf[me] = ps[r // 2]
-    for d in range(1, n):
-        p, device = peer(d)
-        copy = remote(ps.at[p // 4], pbuf.at[me], p_send_sem.at[d], p_recv_sem.at[me], device)
-        copy.start()
-        sends.append(copy)
-    for d in range(1, n):
-        p, device = peer(d)
-        remote(ps.at[0], pbuf.at[p], p_send_sem.at[d], p_recv_sem.at[p], device).wait_recv()
-    pt[...] = pbuf[...].reshape(band, 128).T
+    pbuf[r] = ps[r // 2]
+    for d in range(1, chips):
+        p = lax.rem(r + d, chips)
+        send(remote(ps.at[p // 2], pbuf.at[r], p_send_sem.at[d], p_recv_sem.at[r], {"rows": p, "kern": c}))
+    for d in range(1, chips):
+        p = lax.rem(r + d, chips)
+        remote(ps.at[0], pbuf.at[p], p_send_sem.at[d], p_recv_sem.at[p], {"rows": p, "kern": c}).wait_recv()
+    pt[...] = pbuf[...].reshape(band // 2, 128).T
     base = pl.multiple_of(4 * half * lax.rem(r, 2), 4 * half)
     lhs = jnp.concatenate([pt[pl.ds(base, 2 * half), :], pt[pl.ds(base + 2 * half, 2 * half), :]], axis=1)
-    grad_mask = dot3(lhs, rf[0, :, :full], rf[1, :, :full])
-    out[...] = grad_mask * slope
-
-    for copy in (swap_logits, swap_kernels, swap_weights, swap_x, *sends):
-        copy.wait_send()
+    gm_send[...] = dot3(lhs, gt[0], gt[1])
+    swap_gm = pair(gm_send, gm_recv, 5)
+    send(swap_gm)
+    swap_gm.wait_recv()
+    out[...] = (gm_send[...] + gm_recv[...]) * slope
+    for wait in list(pending):
+        need(wait)
 
 
 def fused_on_device(tables, chips, features, head_weight, kernels, kernel_weights, target):
@@ -395,16 +420,19 @@
     half = row_count // 2
     n = 2 * chips
     vmem = pl.BlockSpec(memory_space=pltpu.VMEM)
-    smem = pl.BlockSpec(memory_space=pltpu.SMEM)
-    anywhere = pl.BlockSpec(memory_space=pl.ANY)
+    hbm = pl.BlockSpec(memory_space=pltpu.HBM)
     dma = pltpu.SemaphoreType.DMA
-    rf, rb, rq, lt, lq, ld = tables
+    rf, rb, rq, lt, lq, ld, gt = tables
     grad_logits = pl.pallas_call(
         fused,
         out_shape=jax.ShapeDtypeStruct((row_count, full), f32),
-        in_specs=[smem, smem, vmem, vmem] + [anywhere] * 7,
+        in_specs=[hbm] * 12,
         out_specs=vmem,
         scratch_shapes=[
+            pltpu.SMEM(head_weight.shape, f32),
+            pltpu.SMEM(kernel_weights.shape, f32),
+            pltpu.VMEM(features.shape, bf16),
+            pltpu.VMEM(target.shape, bf16),
             pltpu.VMEM((2, kpc, 2, band, band), f32),
             pltpu.VMEM(rf.shape, bf16),
             pltpu.VMEM(rb.shape, bf16),
@@ -412,32 +440,37 @@
             pltpu.VMEM(lt.shape[1:], bf16),
             pltpu.VMEM(lq.shape[1:], bf16),
             pltpu.VMEM(ld.shape[1:], bf16),
+            pltpu.VMEM(gt.shape[1:], bf16),
             pltpu.VMEM((row_count, full), f32),
             pltpu.VMEM((row_count, full), f32),
             pltpu.VMEM((2, 8, 128), f32),
             pltpu.VMEM((chips, half, 2 * band), f32),
             pltpu.VMEM((2 * band, band), f32),
             pltpu.VMEM((2 * band, band), f32),
-            pltpu.VMEM((n, 2, band // n, band), f32),
-            pltpu.VMEM((n, 2, band // n, band), f32),
+            pltpu.VMEM((2, chips, 2, band // n, band), f32),
+            pltpu.VMEM((chips, 2, band // n, band), f32),
+            pltpu.VMEM((chips, 2, band // n, band), f32),
+            pltpu.VMEM((chips, 2, band // n, band), f32),
             pltpu.VMEM((chips // 2, band // n, 128), f32),
-            pltpu.VMEM((n, band // n, 128), f32),
-            pltpu.VMEM((128, band), f32),
+            pltpu.VMEM((chips, band // n, 128), f32),
+            pltpu.VMEM((128, band // 2), f32),
             pltpu.VMEM((row_count, full), f32),
-            dma((7,)),
-            dma((4,)),
-            dma((4,)),
+            pltpu.VMEM((row_count, full), f32),
+            pltpu.VMEM((row_count, full), f32),
+            dma((12,)),
+            dma((6,)),
+            dma((6,)),
             dma((chips,)),
             dma((chips,)),
-            dma((n,)),
-            dma((n,)),
-            dma((n,)),
-            dma((n,)),
+            dma((chips,)),
+            dma((chips,)),
+            dma((chips,)),
+            dma((chips,)),
         ],
         compiler_params=pltpu.CompilerParams(
-            collective_id=0, has_side_effects=True, vmem_limit_bytes=32 * 1024 * 1024
+            collective_id=0, has_side_effects=True, vmem_limit_bytes=VMEM_BYTES
         ),
-    )(head_weight, kernel_weights, features, target, kernels, *[jnp.asarray(t) for t in (rf, rb, rq, lt, lq, ld)])
+    )(head_weight, kernel_weights, features, target, kernels, *[jnp.asarray(t) for t in tables])
     return (head_weight[:, None, None] * grad_logits[None]).astype(jnp.bfloat16)
 
 

time: 37.3 us -> 27.3 us (0.73)
  local copies, waits for them, and re-layouts: 10.4 us -> 0.01 us
  other arithmetic: 0.74 us -> 1.5 us
    unnamed x22 -> x2, local copies, waits for them, and re-layouts: 10.4 us -> 0.01 us
    convert_element_type x1, other arithmetic: 0.74 us -> 1.5 us  [fused_on_device(): return (head_weight[:, None, None] * grad_logits[None]).astype(jnp.bfloat16)]
where the time goes in v2:
time: 27.3 us; the launch traced here: 27.1 us
  Pallas kernels  25.6 us (94%)
  other arithmetic  1.5 us (5%)
    pallas_call x1, Pallas kernels, fused_on_device(): pl.pallas_call(fused, out_shape=jax.ShapeDtypeStruct((row_count, full), f...  25.6 us
    convert_element_type x1, other arithmetic, fused_on_device(): return (head_weight[:, None, None] * grad_logits[None]).astype(jnp.bfloat16)  1.5 us

profile of v2, /device:TPU:0, one launch (start us, length us, event | category | flops | bytes accessed | tf_op | source)
XLA Modules:
  0.0 27.1 jit_solution(17652450925494270223)
XLA Ops:
  0.0 0.0 copy-start
  0.0 25.6 %shard_map.118 = f32[32,256]{1,0:T(8,128)} custom-call(f32[8]{0:T(128)} %hw_hbm.1, f32[4]{0:T(128)} %kw_hbm.1, bf16[8,32,256]{2,1,0:T(8,128)(2,1)} %feat_hbm.1, bf16[32,256]{1,0:T(8,128)(2,1)} %tgt_hbm.1, f32[4,2,128,128]{3,2,1,0:T(8,128)} %ker_hbm.1, bf16[2,256,512]{2,1,0:T(8,128)(2,1)} %constant.14.clone.rf_hbm, ...), custom_call_target="tpu_custom_call" | custom-call | tf_op jit(solution)/shard_map/pallas_call | solution.py:426
  25.6 0.0 copy-done
  25.6 1.5 %multiply_convert_fusion = bf16[8,32,256]{2,1,0:T(8,128)(2,1)} fusion(f32[32,256]{1,0:T(8,128)} %shard_map.118, f32[8]{0:T(128)S(1)} %copy-done), kind=kLoop, calls=%fused_computation | loop fusion | flops 131072 | bytes 163872 | tf_op jit(solution)/shard_map/convert_element_type | solution.py:474
Async XLA Ops:
  0.0 25.6 %copy-start = (f32[8]{0:T(128)S(1)}, f32[8]{0:T(128)}, u32[]{:S(2)}) copy-start(f32[8]{0:T(128)} %hw_hbm.1) | copy-start | bytes 100

commit v3 on v2

--- a/solution.py
+++ b/solution.py
@@ -172,14 +172,12 @@
     cos, sin = np.cos(angles), np.sin(angles)
     half = row_count // 2
     rf = np.block([[cos.T, sin.T], [-sin.T, cos.T]])
-    rq = rf.reshape(2 * band_len, 2, chips, row_count).transpose(0, 2, 1, 3).reshape(rf.shape)
+    qt = rf.T.reshape(2, chips, 2, half, 2 * band_len).transpose(0, 2, 1, 3, 4).reshape(2 * full_len, 2 * band_len)
     by_core = lambda t: t.reshape(chips, 2, half, band_len)
-    lt, lq, ld, gt = [], [], [], []
+    lt, lq, ld = [], [], []
     for core in range(2):
         c = by_core(cos)[:, core].reshape(-1, band_len)
         s = by_core(sin)[:, core].reshape(-1, band_len)
-        mine = slice(core * band_len // 2, (core + 1) * band_len // 2)
-        gt.append(np.stack(halves(np.concatenate([cos.T[mine], -sin.T[mine]], axis=0))))
         lt.append(np.stack(halves(np.block([[c.T, s.T], [-s.T, c.T]]))))
     for chip in range(chips):
         for core in range(2):
@@ -190,11 +188,10 @@
     return (
         np.stack(halves(rf)),
         np.stack(halves(rf.T)),
-        np.stack(halves(rq)),
+        np.stack(halves(qt)),
         np.stack(lt),
         np.stack(lq),
         np.stack(ld),
-        np.stack(gt),
     )
 
 
@@ -215,11 +212,11 @@
 
 
 def fused(
-    hw_hbm, kw_hbm, feat_hbm, tgt_hbm, ker_hbm, rf_hbm, rb_hbm, rq_hbm, lt_hbm, lq_hbm, ld_hbm, gt_hbm,
+    hw_hbm, kw_hbm, feat_hbm, tgt_hbm, ker_hbm, rf_hbm, rb_hbm, qt_hbm, lt_hbm, lq_hbm, ld_hbm,
     out,
-    hw, kw, feat, tgt, ker, rf, rb, rq, lt, lq, ld, gt,
-    logit_send, logit_recv, wts, hbuf, x_send, x_recv, gs, g_pair, g_sum, gbuf, ps, pbuf, pt, gm_send, gm_recv, mask_buf,
-    local_sem, pair_send, pair_recv, h_send_sem, h_recv_sem, g_send_sem, g_recv_sem, p_send_sem, p_recv_sem,
+    hw, kw, feat, tgt, ker, rf, rb, qt, lt, lq, ld,
+    logit_send, logit_recv, wts, hbuf, x_send, x_recv, qbuf, gs, g_pair, g_sum, gbuf, final, mask_buf,
+    local_sem, pair_send, pair_recv, h_send_sem, h_recv_sem, g_send_sem, g_recv_sem,
 ):
     chips, half, _ = hbuf.shape
     band = ker.shape[-1]
@@ -227,7 +224,6 @@
     channels = feat.shape[0]
     kpc = ker.shape[1]
     kcount = 2 * kpc
-    n = 2 * chips
     r = lax.axis_index("rows")
     c = lax.axis_index("kern")
     me = 2 * r + c
@@ -261,8 +257,7 @@
     get_lq = local(lq_hbm.at[me], lq, 3)
     get_rf = local(rf_hbm, rf, 4)
     get_ld = local(ld_hbm.at[me], ld, 5)
-    get_rq = local(rq_hbm, rq, 6)
-    get_gt = local(gt_hbm.at[c], gt, 11)
+    get_qt = local(qt_hbm, qt, 6)
 
     need(get_hw)
     need(get_feat)
@@ -374,16 +369,22 @@
             kr, ki = kernel_of(k, 0), kernel_of(k, 1)
             gr = gr + (kr * dr + ki * di)
             gi = gi + (kr * di - ki * dr)
-    gs[:, :, 0] = gr.T.reshape(2, chips, band // n, band)
-    gs[:, :, 1] = gi.T.reshape(2, chips, band // n, band)
-    swap_g = pair(gs.at[1 - c], g_pair, 4)
+    need(get_qt)
+    g_high, g_low = split(jnp.concatenate([gr, gi], axis=0))
+    q = mm(qt[0], g_high) + (mm(qt[1], g_high) + mm(qt[0], g_low))
+    qbuf[...] = jnp.concatenate([q[:full], q[full:]], axis=1).reshape(qbuf.shape)
+
+    def back(core):
+        return dot3(qbuf[core], rf[0, :, :full], rf[1, :, :full]).reshape(chips, half, full)
+
+    gs[...] = back(1 - c)
+    swap_g = pair(gs, g_pair, 4)
     send(swap_g)
-    need(get_rq)
-    need(get_gt)
-    mask = mask_buf[...]
+    g_sum[...] = back(c)
+    mask = mask_buf[pl.ds(pl.multiple_of(half * c, half), half), :]
     slope = mask * (1.0 - mask) * (1.0 / (full * band))
     swap_g.wait_recv()
-    g_sum[...] = gs[c] + g_pair[...]
+    g_sum[...] = g_sum[...] + g_pair[...]
     for d in range(1, chips):
         p = lax.rem(r + d, chips)
         send(remote(g_sum.at[p], gbuf.at[d], g_send_sem.at[d], g_recv_sem.at[d], {"rows": p, "kern": c}))
@@ -392,24 +393,10 @@
         p = lax.rem(r + d, chips)
         remote(g_sum.at[p], gbuf.at[d], g_send_sem.at[d], g_recv_sem.at[d], {"rows": p, "kern": c}).wait_recv()
         g = g + gbuf[d]
-    q = dot3(jnp.concatenate([g[0], g[1]], axis=1), rq[0], rq[1])
-    for j in range(chips // 2):
-        ps[j] = q[:, 128 * j : 128 * (j + 1)]
-    pbuf[r] = ps[r // 2]
-    for d in range(1, chips):
-        p = lax.rem(r + d, chips)
-        send(remote(ps.at[p // 2], pbuf.at[r], p_send_sem.at[d], p_recv_sem.at[r], {"rows": p, "kern": c}))
-    for d in range(1, chips):
-        p = lax.rem(r + d, chips)
-        remote(ps.at[0], pbuf.at[p], p_send_sem.at[d], p_recv_sem.at[p], {"rows": p, "kern": c}).wait_recv()
-    pt[...] = pbuf[...].reshape(band // 2, 128).T
-    base = pl.multiple_of(4 * half * lax.rem(r, 2), 4 * half)
-    lhs = jnp.concatenate([pt[pl.ds(base, 2 * half), :], pt[pl.ds(base + 2 * half, 2 * half), :]], axis=1)
-    gm_send[...] = dot3(lhs, gt[0], gt[1])
-    swap_gm = pair(gm_send, gm_recv, 5)
-    send(swap_gm)
-    swap_gm.wait_recv()
-    out[...] = (gm_send[...] + gm_recv[...]) * slope
+    final[c] = g * slope
+    send(pair(final.at[c], final.at[c], 5))
+    pair(final.at[1 - c], final.at[1 - c], 5).wait_recv()
+    out[...] = final[...].reshape(out.shape)
     for wait in list(pending):
         need(wait)
 
@@ -418,15 +405,14 @@
     channels, row_count, full = features.shape
     kpc, _, band, _ = kernels.shape
     half = row_count // 2
-    n = 2 * chips
     vmem = pl.BlockSpec(memory_space=pltpu.VMEM)
     hbm = pl.BlockSpec(memory_space=pltpu.HBM)
     dma = pltpu.SemaphoreType.DMA
-    rf, rb, rq, lt, lq, ld, gt = tables
+    rf, rb, qt, lt, lq, ld = tables
     grad_logits = pl.pallas_call(
         fused,
         out_shape=jax.ShapeDtypeStruct((row_count, full), f32),
-        in_specs=[hbm] * 12,
+        in_specs=[hbm] * 11,
         out_specs=vmem,
         scratch_shapes=[
             pltpu.SMEM(head_weight.shape, f32),
@@ -436,32 +422,26 @@
             pltpu.VMEM((2, kpc, 2, band, band), f32),
             pltpu.VMEM(rf.shape, bf16),
             pltpu.VMEM(rb.shape, bf16),
-            pltpu.VMEM(rq.shape, bf16),
+            pltpu.VMEM(qt.shape, bf16),
             pltpu.VMEM(lt.shape[1:], bf16),
             pltpu.VMEM(lq.shape[1:], bf16),
             pltpu.VMEM(ld.shape[1:], bf16),
-            pltpu.VMEM(gt.shape[1:], bf16),
             pltpu.VMEM((row_count, full), f32),
             pltpu.VMEM((row_count, full), f32),
             pltpu.VMEM((2, 8, 128), f32),
             pltpu.VMEM((chips, half, 2 * band), f32),
             pltpu.VMEM((2 * band, band), f32),
             pltpu.VMEM((2 * band, band), f32),
-            pltpu.VMEM((2, chips, 2, band // n, band), f32),
-            pltpu.VMEM((chips, 2, band // n, band), f32),
-            pltpu.VMEM((chips, 2, band // n, band), f32),
-            pltpu.VMEM((chips, 2, band // n, band), f32),
-            pltpu.VMEM((chips // 2, band // n, 128), f32),
-            pltpu.VMEM((chips, band // n, 128), f32),
-            pltpu.VMEM((128, band // 2), f32),
+            pltpu.VMEM((2, chips * half, 2 * band), f32),
+            pltpu.VMEM((chips, half, full), f32),
+            pltpu.VMEM((chips, half, full), f32),
+            pltpu.VMEM((chips, half, full), f32),
+            pltpu.VMEM((chips, half, full), f32),
+            pltpu.VMEM((2, half, full), f32),
             pltpu.VMEM((row_count, full), f32),
-            pltpu.VMEM((row_count, full), f32),
-            pltpu.VMEM((row_count, full), f32),
-            dma((12,)),
+            dma((11,)),
             dma((6,)),
             dma((6,)),
-            dma((chips,)),
-            dma((chips,)),
             dma((chips,)),
             dma((chips,)),
             dma((chips,)),

time: 27.3 us -> 24.7 us (0.905)
  Pallas kernels: 25.6 us -> 23 us
    pallas_call x1, Pallas kernels: 25.6 us -> 23 us  [fused_on_device(): pl.pallas_call(fused, out_shape=jax.ShapeDtypeStruct((row_count, full), f...]
where the time goes in v3:
time: 24.7 us; the launch traced here: 24.5 us
  Pallas kernels  23 us (93%)
  other arithmetic  1.5 us (6%)
    pallas_call x1, Pallas kernels, fused_on_device(): pl.pallas_call(fused, out_shape=jax.ShapeDtypeStruct((row_count, full), f...  23 us
    convert_element_type x1, other arithmetic, fused_on_device(): return (head_weight[:, None, None] * grad_logits[None]).astype(jnp.bfloat16)  1.5 us

profile of v3, /device:TPU:0, one launch (start us, length us, event | category | flops | bytes accessed | tf_op | source)
XLA Modules:
  0.0 24.5 jit_solution(7586597196875620174)
XLA Ops:
  0.0 0.0 copy-start
  0.0 23.0 %shard_map.109 = f32[32,256]{1,0:T(8,128)} custom-call(f32[8]{0:T(128)} %hw_hbm.1, f32[4]{0:T(128)} %kw_hbm.1, bf16[8,32,256]{2,1,0:T(8,128)(2,1)} %feat_hbm.1, bf16[32,256]{1,0:T(8,128)(2,1)} %tgt_hbm.1, f32[4,2,128,128]{3,2,1,0:T(8,128)} %ker_hbm.1, bf16[2,256,512]{2,1,0:T(8,128)(2,1)} %constant.12.clone.rf_hbm, ...), custom_call_target="tpu_custom_call" | custom-call | tf_op jit(solution)/shard_map/pallas_call | solution.py:412
  23.0 0.0 copy-done
  23.1 1.5 %multiply_convert_fusion = bf16[8,32,256]{2,1,0:T(8,128)(2,1)} fusion(f32[32,256]{1,0:T(8,128)} %shard_map.109, f32[8]{0:T(128)S(1)} %copy-done), kind=kLoop, calls=%fused_computation | loop fusion | flops 131072 | bytes 163872 | tf_op jit(solution)/shard_map/convert_element_type | solution.py:454
Async XLA Ops:
  0.0 23.0 %copy-start = (f32[8]{0:T(128)S(1)}, f32[8]{0:T(128)}, u32[]{:S(2)}) copy-start(f32[8]{0:T(128)} %hw_hbm.1) | copy-start | bytes 100
